TPU v7x, 32 devices: a whole 2x2x4 slice. The times are simulated.
32 devices in a mesh: det: 8 (over z, x), tm: 4 (over y, core).
Axes of the slice: x: 2, y: 2, z: 4, core: 2. Of those that a mesh axis runs over, the one named last changes fastest.
Arguments:
- x_map: float32 [3, 4096, 256], P(None, ('det', 'tm')), may hold values from -6 to 6
- r_map: float32 [3, 4096, 256], P(None, ('det', 'tm')), may hold values from -45 to 45
- p_map: float32 [3, 4096, 256], P(None, ('det', 'tm')), may hold values from -45 to 45
- pointing: int32 [32, 16384], P('det', 'tm'), may hold values from 0 to 2047
- pol_angle: float32 [32, 16384], P('det', 'tm'), may hold values from -3.140625 to 3.140625
- noise_filter: bfloat16 [32, 8192], P('det'), may hold values from -2 to 2
- block_list: int32 [8, 128, 8], P('det', 'tm'), may hold values from 0 to 4095, as said below
- block_home: int32 [4096], replicated, may hold values from 0 to 4095, as said below
Outputs:
- x_next: float32 [3, 4096, 256], P(None, ('det', 'tm'))
- r_next: float32 [3, 4096, 256], P(None, ('det', 'tm'))
- p_next: float32 [3, 4096, 256], P(None, ('det', 'tm'))
Inputs may be any that keep to these rules, and one draw needn't show every extreme that they name: Block b is stored at row block_home[b] of the maps, a permutation. `block_list`: repeats allowed. The 256 entries of one device's lists name at most 16 blocks stored on any one device (counted with repeats), exactly 16 on some; one device's stored blocks are named 16 times by every device's lists.
All inputs are finite; a program needn't handle non-finite values.
Results may differ from a plain program's by a relative error of at most 0.0034.
The roundings to bfloat16 on the way count: a program that leaves them out, or rounds other values in their place, can miss the bound.
Values may be sent and summed in bfloat16 or wider, within the bound.
A program may use at most 128 MiB of HBM per device.

v0:
```python
import jax
import jax.numpy as jnp
from jax import lax
from jax.sharding import PartitionSpec as P


def with_halo(block, sides, width):
    for axis, dim in sides:
        count = lax.axis_size(axis)
        forward = [(i, i + 1) for i in range(count - 1)]
        backward = [(target, source) for source, target in forward]
        low = lax.ppermute(
            lax.slice_in_dim(block, block.shape[dim] - width, None, axis=dim), axis, forward
        )
        high = lax.ppermute(lax.slice_in_dim(block, 0, width, axis=dim), axis, backward)
        block = jnp.concatenate([low, block, high], axis=dim)
    return block


def apply_filter(padded, noise_filter, samples):
    tap_count = noise_filter.shape[1]
    window_len = tap_count + 128
    windows = samples // 128
    span_rows = tap_count // 128 + 1

    def one_detector(series, coeffs):
        extended = jnp.concatenate([coeffs, jnp.zeros((129,), coeffs.dtype)])
        toeplitz = jnp.tile(extended, 128)[: 128 * window_len].reshape(128, window_len)
        pieces = series.reshape(-1, 128)
        framed = jnp.stack(
            [pieces[offset_rows : offset_rows + windows] for offset_rows in range(span_rows)],
            axis=1,
        )
        framed = framed.reshape(windows, window_len)
        result = lax.dot_general(
            framed, toeplitz, (((1,), (1,)), ((), ())), preferred_element_type=jnp.float32
        )
        return result.reshape(samples)

    groups = padded.shape[0] // 4

    def one_group(bundle):
        return jax.vmap(one_detector)(bundle[0], bundle[1])

    output = lax.map(
        one_group, (padded.reshape(groups, 4, -1), noise_filter.reshape(groups, 4, tap_count))
    )
    return output.reshape(-1, samples)


def body(x_map, r_map, p_map, pointing, pol_angle, noise_filter, block_list, block_home):
    det_count = lax.axis_size("det")
    time_count = lax.axis_size("tm")
    devices = det_count * time_count
    list_len = block_list.shape[2]
    per_device = block_list.shape[1] * list_len
    capacity = 2 * per_device // devices
    slot_count = devices * capacity
    blocks_here = p_map.shape[1]
    pixels = p_map.shape[2]
    wanted = block_list.reshape(per_device)
    stored = jnp.take(block_home, wanted)
    owner_index = stored // blocks_here
    slot_of = stored % blocks_here
    member = (owner_index[:, None] == jnp.arange(devices, dtype=jnp.int32)[None, :]).astype(
        jnp.int32
    )
    ranking = jnp.sum((jnp.cumsum(member, axis=0) - 1) * member, axis=1)
    send_place = owner_index * capacity + ranking
    request = jnp.full((slot_count,), -1, jnp.int32).at[send_place].set(slot_of)
    asked_slots = lax.all_to_all(request, ("det", "tm"), split_axis=0, concat_axis=0, tiled=True)
    present = asked_slots >= 0
    answer = jnp.where(present[None, :, None], p_map[:, jnp.maximum(asked_slots, 0), :], 0.0)
    fetched = lax.all_to_all(answer, ("det", "tm"), split_axis=1, concat_axis=1, tiled=True)
    local_map = fetched[:, send_place, :].reshape(3, per_device * pixels)
    samples = pointing.shape[1]
    block_span = samples // block_list.shape[1]
    time_block = jnp.arange(samples, dtype=jnp.int32) // block_span
    address = time_block[None, :] * (list_len * pixels) + pointing
    cosine = jnp.cos(2.0 * pol_angle)
    sine_part = jnp.sin(2.0 * pol_angle)
    signal = (
        local_map[0][address] + cosine * local_map[1][address] + sine_part * local_map[2][address]
    ).astype(jnp.bfloat16)
    tap_count = noise_filter.shape[1]
    padded = with_halo(signal, (("tm", 1),), tap_count // 2)
    rounded = apply_filter(padded, noise_filter, samples).astype(jnp.bfloat16)
    filtered = lax.optimization_barrier(rounded).astype(jnp.float32)
    terms = jnp.stack([filtered, filtered * cosine, filtered * sine_part]).reshape(3, -1)
    partial_value = (
        jnp.zeros((3, per_device * pixels), jnp.float32).at[:, address.reshape(-1)].add(terms)
    )
    outgoing = (
        jnp.zeros((3, slot_count, pixels), jnp.float32)
        .at[:, send_place, :]
        .set(partial_value.reshape(3, per_device, pixels))
    )
    returned = lax.all_to_all(outgoing, ("det", "tm"), split_axis=1, concat_axis=1, tiled=True)
    selector = (asked_slots[:, None] == jnp.arange(blocks_here, dtype=jnp.int32)[None, :]).astype(
        jnp.float32
    )
    image = jnp.einsum("sk,csb->ckb", selector, returned, precision=lax.Precision.HIGHEST)
    norm_old = lax.psum(jnp.sum(r_map * r_map), ("det", "tm"))
    curvature = lax.psum(jnp.sum(p_map * image), ("det", "tm"))
    step_size = norm_old / curvature
    r_next = r_map - step_size * image
    norm_new = lax.psum(jnp.sum(r_next * r_next), ("det", "tm"))
    x_next = x_map + step_size * p_map
    p_next = r_next + norm_new / norm_old * p_map
    return (x_next, r_next, p_next)


def solution(mesh):
    return jax.shard_map(
        body,
        mesh=mesh,
        in_specs=(
            P(None, ("det", "tm"), None),
            P(None, ("det", "tm"), None),
            P(None, ("det", "tm"), None),
            P("det", "tm"),
            P("det", "tm"),
            P("det", None),
            P("det", "tm", None),
            P(),
        ),
        out_specs=(
            P(None, ("det", "tm"), None),
            P(None, ("det", "tm"), None),
            P(None, ("det", "tm"), None),
        ),
        check_vma=False,
    )
```

profile of v0, /device:TPU:0, one launch (start us, length us, event | category | flops | bytes accessed | tf_op | source)
XLA Modules:
  0.0 697.4 jit_solution(10474817990767673283)
XLA Ops:
  1.8 1.7 gather_fusion
  4.5 1.4 scatter_custom_fusion
  6.0 14.2 %all_to_all.22 = s32[32,16,1]{1,2,0:T(1,128)S(1)} all-to-all(s32[32,16,1]{1,2,0:T(1,128)S(1)} %bitcast.432), channel_id=1, replica_groups=mesh['det'=8,'tm'=4] {'det','tm'}, dimensions={0} | all-to-all | bytes 4096 | tf_op jit(solution)/shard_map/all_to_all | solution.py:71
  22.2 3.7 gather_fusion.1
  26.0 2.4 copy.112
  28.5 2.9 all-to-all-start.1
  32.8 47.3 %all-to-all-done.1 = f32[3,512,256]{2,0,1:T(4,128)S(1)} async-done(((f32[3,512,256]{2,0,1:T(4,128)}), f32[3,512,256]{2,0,1:T(4,128)S(1)}, u32[]{:S(2)}, u32[]{:S(2)}) %all-to-all-start.1) | async-done | bytes 1572896 | tf_op jit(solution)/shard_map/all_to_all | solution.py:74
  80.1 1.3 gather_fusion.2
  81.9 90.8 %gather_fusion.3 = f32[16384]{0:T(1024)S(1)} fusion(f32[65536]{0:T(1024)S(1)} %bitcast.354, s32[16384]{0:T(1024)} %broadcast_clamp_fusion), kind=kCustom, calls=%fused_computation.3 | custom fusion | bytes 196608 | tf_op jit(solution)/shard_map/gather | solution.py:83
  172.8 90.5 %gather_fusion.4 = f32[16384]{0:T(1024)S(1)} fusion(f32[65536]{0:T(1024)S(1)} %bitcast.353, s32[16384]{0:T(1024)S(1)} %copy-done.5), kind=kCustom, calls=%fused_computation.4 | custom fusion | bytes 196608 | tf_op jit(solution)/shard_map/gather | solution.py:83
  263.4 90.5 %gather_fusion.5 = f32[16384]{0:T(1024)S(1)} fusion(f32[65536]{0:T(1024)S(1)} %bitcast.352, s32[16384]{0:T(1024)S(1)} %copy-done.5), kind=kCustom, calls=%fused_computation.5 | custom fusion | bytes 196608 | tf_op jit(solution)/shard_map/gather | solution.py:83
  354.5 1.5 collective-permute-start
  356.0 1.5 collective-permute-start.1
  357.6 3.9 tile.14
  361.5 18.0 %reshape.389 = bf16[4260352]{0:T(1024)(128)(2,1)} reshape(bf16[4,128,8321]{2,1,0:T(8,128)(2,1)} %tile.14) | data formatting | bytes 17041408
  379.5 15.0 %tile.15 = bf16[4,1065088]{1,0:T(4,128)(2,1)} reshape(bf16[4260352]{0:T(1024)(128)(2,1)} %reshape.389) | data formatting | bytes 17041408 | tf_op jit(solution)/shard_map/while/body/eval_jaxpr/vmap()/tile | solution.py:28
  396.0 1.9 slice-done
  397.9 3.0 fusion.17
  401.8 5.3 copy.114
  407.1 100.8 %scatter_custom_fusion.1 = f32[3,65536]{0,1:T(8,128)} fusion(s32[16384]{0:T(1024)S(1)} %bitcast.431, f32[16384,3]{1,0:T(8,128)} %copy.114, f32[]{:T(128)} %constant.81.clone.1), kind=kCustom, calls=%fused_computation.9 | custom fusion | flops 49152 | bytes 786944 | tf_op jit(solution)/shard_map/scatter-add | solution.py:91
  507.9 17.9 %copy.115 = f32[3,256,256]{2,0,1:T(4,128)S(1)} copy(f32[3,256,256]{0,2,1:T(8,128)} %bitcast.355) | data formatting | bytes 1572864 | tf_op jit(solution)/shard_map/reshape | solution.py:96
  525.8 1.6 broadcast_in_dim.31
  527.4 23.9 %scatter_fusion = f32[3,512,256]{2,0,1:T(4,128)} fusion(f32[3,512,256]{2,0,1:T(4,128)} %broadcast_in_dim.31, s32[256]{0:T(256)S(1)} %bitcast.436, f32[256,3,256]{2,1,0:T(4,128)S(1)} %bitcast.422), kind=kCustom, calls=%fused_computation.8 | custom fusion | bytes 2360320 | tf_op jit(solution)/shard_map/scatter | solution.py:96
  551.4 6.7 all-to-all-start.2
  559.2 1.9 copy.119
  561.8 45.1 %all-to-all-done.2 = f32[3,512,256]{2,0,1:T(4,128)S(1)} async-done(((f32[3,512,256]{2,0,1:T(4,128)}), f32[3,512,256]{2,0,1:T(4,128)S(1)}, u32[]{:S(2)}, u32[]{:S(2)}) %all-to-all-start.2) | async-done | bytes 1572896 | tf_op jit(solution)/shard_map/all_to_all | solution.py:98
  606.9 2.9 multiply_reduce_fusion.1
  609.8 38.4 %all-reduce.1 = (f32[]{:T(128)}, f32[]{:T(128)}) all-reduce(f32[]{:T(128)} %multiply_reduce_fusion.2, f32[]{:T(128)} %get-tuple-element.41), channel_id=1, replica_groups=mesh['det'=8,'tm'=4] {'det','tm'}, use_global_device_ids=true, to_apply=%region_1.2 | all-reduce | flops 2 | bytes 16 | tf_op jit(solution)/shard_map/psum | solution.py:103
  649.4 1.9 multiply_reduce_fusion
  651.3 41.4 %psum.23 = f32[]{:T(128)} all-reduce(f32[]{:T(128)} %get-tuple-element.28), channel_id=1, replica_groups=mesh['det'=8,'tm'=4] {'det','tm'}, use_global_device_ids=true, to_apply=%region_11.12 | all-reduce | flops 1 | bytes 8 | tf_op jit(solution)/shard_map/psum | solution.py:107
  694.1 0.9 copy.123
  695.1 0.9 copy.122
  (147 shorter events, 11.9 us)
Async XLA Ops:
  0.6 1.1 copy-start
  0.6 21.5 %copy-start.2 = (f32[3,128,256]{2,1,0:T(8,128)S(1)}, f32[3,128,256]{2,1,0:T(8,128)}, u32[]{:S(2)}) copy-start(f32[3,128,256]{2,1,0:T(8,128)} %param.10) | copy-start | bytes 1179652
  4.5 27.6 %copy-start.12 = (s32[256,1]{0,1:T(1,128)}, s32[256,1]{0,1:T(1,128)S(1)}, u32[]{:S(2)}) copy-start(s32[256,1]{0,1:T(1,128)S(1)} %compare_select_fusion.2) | copy-start | bytes 3076
  21.6 0.6 copy-start.10
  28.5 2.9 copy-start.8
  28.5 51.6 %all-to-all-start.1 = ((f32[3,512,256]{2,0,1:T(4,128)}), f32[3,512,256]{2,0,1:T(4,128)S(1)}, u32[]{:S(2)}, u32[]{:S(2)}) async-start(f32[3,512,256]{2,0,1:T(4,128)} %copy.112), calls=%async_computation.1 | async-start | bytes 4194304 | tf_op jit(solution)/shard_map/all_to_all | solution.py:74
  81.9 90.8 %copy-start.5 = (s32[16384]{0:T(1024)S(1)}, s32[16384]{0:T(1024)}, u32[]{:S(2)}) copy-start(s32[16384]{0:T(1024)} %broadcast_clamp_fusion) | copy-start | bytes 196612
  263.3 90.6 %copy-start.6 = (f32[4,4096]{1,0:T(4,128)S(1)}, f32[4,4096]{1,0:T(4,128)}, u32[]{:S(2)}) copy-start(f32[4,4096]{1,0:T(4,128)} %param.12) | copy-start | bytes 196612
  263.3 94.1 %copy-start.7 = (s32[1,1,4,4096]{3,1,2,0:T(1,128)S(1)}, s32[1,1,4,4096]{3,1,2,0:T(1,128)}, u32[]{:S(2)}) copy-start(s32[1,1,4,4096]{3,1,2,0:T(1,128)} %copy.127) | copy-start | bytes 196612
  263.4 94.2 %copy-start.9 = (bf16[4,8192]{1,0:T(4,128)(2,1)S(1)}, bf16[4,8192]{1,0:T(4,128)(2,1)}, u32[]{:S(2)}) copy-start(bf16[4,8192]{1,0:T(4,128)(2,1)} %param.13) | copy-start | bytes 196612
  354.5 40.0 %collective-permute-start = (bf16[4,4096]{1,0:T(4,128)(2,1)S(1)}, bf16[4,4096]{1,0:T(4,128)(2,1)S(1)}, u32[]{:S(2)}, u32[]{:S(2)}) collective-permute-start(bf16[4,4096]{1,0:T(4,128)(2,1)S(1)} %add_convert_fusion), channel_id=1, source_target_pairs={{0,1},{1,2},{2,3},{4,5},{5,6},{6,7},{8,9},{9,10},{10,11},{12,13},{... | collective-permute-start | bytes 98312 | tf_op jit(solution)/shard_map/ppermute | solution.py:12
  356.0 38.4 %collective-permute-start.1 = (bf16[4,4096]{1,0:T(4,128)(2,1)S(1)}, bf16[4,4096]{1,0:T(4,128)(2,1)S(1)}, u32[]{:S(2)}, u32[]{:S(2)}) collective-permute-start(bf16[4,4096]{1,0:T(4,128)(2,1)S(1)} %add_convert_fusion), channel_id=1, source_target_pairs={{1,0},{2,1},{3,2},{5,4},{6,5},{7,6},{9,8},{10,9},{11,10},{13,12},{... | collective-permute-start | bytes 98312 | tf_op jit(solution)/shard_map/ppermute | solution.py:15
  394.4 3.4 slice-start
  507.9 19.6 %copy-start.13 = (s32[256,1]{0,1:T(1,128)S(1)}, s32[256,1]{0,1:T(1,128)}, u32[]{:S(2)}) copy-start(s32[256,1]{0,1:T(1,128)} %copy-done.12) | copy-start | bytes 3076
  551.4 6.9 copy-start.3
  551.4 55.5 %all-to-all-start.2 = ((f32[3,512,256]{2,0,1:T(4,128)}), f32[3,512,256]{2,0,1:T(4,128)S(1)}, u32[]{:S(2)}, u32[]{:S(2)}) async-start(f32[3,512,256]{2,0,1:T(4,128)} %scatter_fusion), calls=%async_computation.2 | async-start | bytes 4194304 | tf_op jit(solution)/shard_map/all_to_all | solution.py:98
  558.1 48.8 %copy-start.11 = (s32[512]{0:T(512)S(1)}, s32[512]{0:T(512)}, u32[]{:S(2)}) copy-start(s32[512]{0:T(512)} %copy-done.10) | copy-start | bytes 6148
  561.8 133.2 %copy-start.4 = (f32[3,128,256]{1,2,0:T(8,128)S(1)}, f32[3,128,256]{1,2,0:T(8,128)}, u32[]{:S(2)}) copy-start(f32[3,128,256]{1,2,0:T(8,128)} %copy.119) | copy-start | bytes 1179652
  694.1 2.8 copy-start.1
where the time goes:
time: 706 us; the launch traced here: 697 us
  local copies, waits for them, and re-layouts  381 us (54%)
  other arithmetic  107 us (15%)
  blocking collectives  94.1 us (13%)
  waiting for transfers between devices  92.4 us (13%)
  starting transfers between devices  12.6 us (2%)
    scatter-add x1, other arithmetic, body(): jnp.zeros((3, per_device * pixels), jnp.float32).at[:, address.reshape(-1)]  101 us
    gather x2, local copies, waits for them, and re-layouts, body(): local_map[0][address] + cosine * local_map[1][address]  90.8 us
    gather x2, local copies, waits for them, and re-layouts, body(): local_map[1][address]  90.6 us
    gather x2, local copies, waits for them, and re-layouts, body(): local_map[2][address]  90.6 us
    all_to_all x1, waiting for transfers between devices, body(): lax.all_to_all(answer, ('det', 'tm'), split_axis=1, concat_axis=1, tiled=...  47.3 us
    all_to_all x1, waiting for transfers between devices, body(): lax.all_to_all(outgoing, ('det', 'tm'), split_axis=1, concat_axis=1, tile...  45.1 us
    psum x1, blocking collectives, body(): norm_new = lax.psum(jnp.sum(r_next * r_next), ('det', 'tm'))  41.4 us
    psum x1, blocking collectives, body(): norm_old = lax.psum(jnp.sum(r_map * r_map), ('det', 'tm'))  38.4 us
  transfers between devices with their start and end apart: 4, of which 2 were waited for; matrix products, arithmetic and copies ran while one was open for 6% of the time, Pallas kernels for 0%

commit v1 on v0

v1 whole, which is shorter than its diff:
```python
import functools

import jax
import jax.numpy as jnp
from jax import lax
from jax.experimental import pallas as pl
from jax.experimental.pallas import tpu as pltpu
from jax.sharding import PartitionSpec as P

F32 = jnp.float32
BF16 = jnp.bfloat16
NN = (((1,), (0,)), ((), ()))
NT = (((1,), (1,)), ((), ()))
TN = (((0,), (0,)), ((), ()))


def dot(a, b, dims):
    return lax.dot_general(a, b, dims, preferred_element_type=F32)


def iota(shape, dim):
    return lax.broadcasted_iota(jnp.int32, shape, dim)


def onehot(cond):
    return jnp.where(cond, 1.0, 0.0).astype(BF16)


def quantize(value):
    largest = jnp.max(jnp.abs(value), axis=1, keepdims=True)
    exponent = jnp.ceil(jnp.log2(jnp.clip(largest, 1e-30, 1e30)))
    whole = jnp.clip(jnp.round(value * jnp.exp2(15.0 - exponent)), -32767.0, 32767.0)
    high = jnp.floor(whole * (1.0 / 256.0))
    return high.astype(BF16), (whole - 256.0 * high).astype(BF16), exponent


def split(words):
    whole = words.astype(jnp.int32).astype(F32)
    high = jnp.floor(whole * (1.0 / 256.0))
    return high, whole - 256.0 * high


def exponent_lanes(exponents):
    rows = exponents[0].shape[0]
    lane = iota((rows, 128), 1)
    out = jnp.zeros((rows, 128), F32)
    for c, e in enumerate(exponents):
        out = jnp.where(lane == c, e, out)
    return out.astype(BF16)


def kernel(
    n_det, n_tm, cap,
    x_ref, r_ref, p_ref, point_ref, angle_ref, filter_ref, wanted_ref, home_ref,
    xo_ref, ro_ref, po_ref,
    ask_out, ask_in, ans_out, ans_in, ret_out, ret_in, red_out, red_in,
    place_ref, hot_ref, toep_ref, frames_ref, pt_ref, cos_ref, sin_ref, sig_ref, y_ref,
    series_ref, halo_out, halo_low, halo_high, lmh_ref, lml_ref, part_ref, image_ref,
    send_sem, recv_sem, halo_send, halo_recv,
):
    n = n_det * n_tm
    det, tm = lax.axis_index("det"), lax.axis_index("tm")
    me = det * n_tm + tm
    comps, blocks, pixels = p_ref.shape
    dets, samples = point_ref.shape
    entries = wanted_ref.shape[1]
    slots = n * cap
    tblocks = samples // 128
    per_block = entries // tblocks
    taps = filter_ref.shape[1]
    tap_rows = taps // 128
    wide = dets * 128
    data = comps * pixels

    def device(index):
        return (index // n_tm, index % n_tm)

    barrier = pltpu.get_barrier_semaphore()

    def greet(k, c):
        pl.semaphore_signal(
            barrier, inc=1, device_id=device((me + k) % n), device_id_type=pl.DeviceIdType.MESH
        )
        return c

    lax.fori_loop(1, n, greet, 0)

    def send_copy(stage, out, into, peer):
        return pltpu.make_async_remote_copy(
            src_ref=out, dst_ref=into.at[me], send_sem=send_sem.at[stage, peer],
            recv_sem=recv_sem.at[stage, me], device_id=device(peer),
            device_id_type=pl.DeviceIdType.MESH,
        )

    def recv_copy(stage, out, into, peer):
        return pltpu.make_async_remote_copy(
            src_ref=out, dst_ref=into.at[peer], send_sem=send_sem.at[stage, peer],
            recv_sem=recv_sem.at[stage, peer], device_id=device(peer),
            device_id_type=pl.DeviceIdType.MESH,
        )

    def send_all(stage, source, into):
        def step(k, c):
            peer = (me + k) % n
            send_copy(stage, source(peer), into, peer).start()
            return c

        lax.fori_loop(1, n, step, 0)

    def wait_all(stage, source, into):
        def step(k, c):
            peer = (me + n - k) % n
            recv_copy(stage, source(peer), into, peer).wait_recv()
            return c

        lax.fori_loop(1, n, step, 0)

    def wait_sent(stage, source, into):
        def step(k, c):
            peer = (me + k) % n
            send_copy(stage, source(peer), into, peer).wait_send()
            return c

        lax.fori_loop(1, n, step, 0)

    wanted = wanted_ref[...]
    home = home_ref[...]
    home_rows = home.shape[0]
    low_hot = onehot(iota((128, entries), 0) == (wanted & 127))
    row_mask = iota((home_rows, entries), 0) == (wanted >> 7)
    owner_table = (home // blocks).astype(F32).astype(BF16)
    slot_table = (home % blocks).astype(F32).astype(BF16)

    def lookup(table):
        return jnp.sum(jnp.where(row_mask, dot(table, low_hot, NN), 0.0), axis=0, keepdims=True)

    owner = lookup(owner_table).astype(jnp.int32)
    slot = lookup(slot_table).astype(jnp.int32)
    member = iota((n, entries), 0) == owner
    earlier = onehot(iota((entries, entries), 0) < iota((entries, entries), 1))
    rank = jnp.sum(
        jnp.where(member, dot(onehot(member), earlier, NN), 0.0), axis=0, keepdims=True
    ).astype(jnp.int32)
    place_ref[...] = onehot(iota((slots, entries), 0) == owner * cap + rank)
    slot_hot = onehot(iota((blocks, entries), 0) == slot)
    ask_out[...] = dot(place_ref[...], slot_hot, NT).astype(BF16).reshape(n, cap, blocks)
    pl.semaphore_wait(barrier, n - 1)
    send_all(0, lambda d: ask_out.at[d], ask_in)
    ask_in[pl.ds(me, 1)] = ask_out[pl.ds(me, 1)]

    pieces = [quantize(p_ref[c]) for c in range(comps)]
    scales = exponent_lanes([e for _, _, e in pieces])

    wait_all(0, lambda d: ask_out.at[d], ask_in)
    asked = ask_in[...].reshape(slots, blocks)

    def place_words(selector, high, low):
        return (256.0 * dot(selector, high, NN) + dot(selector, low, NN)).astype(jnp.int32)

    def fill(buffer, selector, quantized, scale_lanes):
        for c, (high, low, _) in enumerate(quantized):
            words = place_words(selector, high, low).astype(jnp.int16)
            buffer[:, :, c * pixels : (c + 1) * pixels] = words.reshape(n, cap, pixels)
        words = dot(selector, scale_lanes, NN).astype(jnp.int32).astype(jnp.int16)
        buffer[:, :, data : data + 128] = words.reshape(n, cap, 128)

    fill(ans_out, asked, pieces, scales)
    send_all(1, lambda d: ans_out.at[d], ans_in)
    ans_in[pl.ds(me, 1)] = ans_out[pl.ds(me, 1)]

    for b in range(tblocks):
        for d in range(dets):
            here = slice(d * 128, (d + 1) * 128)
            pt_ref[b : b + 1, here] = point_ref[d : d + 1, b * 128 : (b + 1) * 128]
            cos_ref[b : b + 1, here] = angle_ref[d : d + 1, b * 128 : (b + 1) * 128]
    twice = 2.0 * cos_ref[...]
    cos_ref[...] = jnp.cos(twice)
    sin_ref[...] = jnp.sin(twice)

    def make_hot(b, c):
        pixel = pt_ref[pl.ds(b, 1), :] & (pixels - 1)
        hot_ref[b] = onehot(iota((pixels, wide), 0) == pixel)
        return c

    lax.fori_loop(0, tblocks, make_hot, 0)
    upper = iota((128, 128), 1) >= iota((128, 128), 0)

    def turned(tile):
        full = jnp.broadcast_to(tile.astype(F32), (128, 128))
        return pltpu.roll(full, 0, 1, stride=1, stride_axis=0)

    def make_toeplitz(b, before):
        lanes = pl.ds(pl.multiple_of(b * 128, 128), 128)
        now = []
        taps_here = filter_ref[:, lanes].astype(F32)
        for d in range(dets):
            tile = turned(taps_here[d : d + 1, :])
            toep_ref[d, :, lanes] = jnp.where(upper, tile, before[d]).astype(BF16)
            now.append(tile)
        return tuple(now)

    zero = jnp.zeros((128, 128), F32)
    last = lax.fori_loop(0, tap_rows, make_toeplitz, (zero,) * dets)
    for d in range(dets):
        toep_ref[d, :, taps : taps + 128] = jnp.where(upper, 0.0, last[d]).astype(BF16)

    wait_all(1, lambda d: ans_out.at[d], ans_in)

    words = ans_in[:, :, data : data + 128].reshape(slots, 128)
    place = place_ref[...]
    exps = dot(place, words.astype(jnp.int32).astype(F32).astype(BF16), TN)
    for c in range(comps):
        high, low = split(ans_in[:, :, c * pixels : (c + 1) * pixels].reshape(slots, pixels))
        scale = jnp.exp2(exps[:, c : c + 1] - 15.0)
        lmh_ref[c] = dot(place, high.astype(BF16), TN) * (256.0 * scale)
        lml_ref[c] = dot(place, low.astype(BF16), TN) * scale

    def entry_mask(b):
        return iota((per_block, wide), 0) == (pt_ref[pl.ds(b, 1), :] // pixels)

    def scan_signal(b, carry):
        rows = pl.ds(pl.multiple_of(b * per_block, per_block), per_block)
        table = jnp.concatenate(
            [ref[c, rows, :] for c in range(comps) for ref in (lmh_ref, lml_ref)], axis=0
        ).astype(BF16)
        seen = dot(table, hot_ref[b], NN)
        parts = [
            seen[2 * c * per_block : (2 * c + 1) * per_block]
            + seen[(2 * c + 1) * per_block : (2 * c + 2) * per_block]
            for c in range(comps)
        ]
        value = (
            parts[0] + cos_ref[pl.ds(b, 1), :] * parts[1] + sin_ref[pl.ds(b, 1), :] * parts[2]
        )
        sig_ref[pl.ds(b, 1), :] = jnp.sum(
            jnp.where(entry_mask(b), value, 0.0), axis=0, keepdims=True
        )
        return carry

    lax.fori_loop(0, tblocks, scan_signal, 0, unroll=4)
    halo_out[...] = sig_ref[...].astype(BF16)

    def halo(side, target, buffer):
        return pltpu.make_async_remote_copy(
            src_ref=halo_out, dst_ref=buffer, send_sem=halo_send.at[side],
            recv_sem=halo_recv.at[side], device_id=(det, target),
            device_id_type=pl.DeviceIdType.MESH,
        )

    to_right = halo(0, (tm + 1) % n_tm, halo_low)
    to_left = halo(1, (tm + n_tm - 1) % n_tm, halo_high)

    @pl.when(tm < n_tm - 1)
    def _():
        to_right.start()

    @pl.when(tm > 0)
    def _():
        to_left.start()

    series_ref[tblocks : 2 * tblocks, :] = halo_out[...].astype(F32)

    @pl.when(tm > 0)
    def _():
        to_right.wait_recv()
        series_ref[0:tblocks, :] = halo_low[...].astype(F32)

    @pl.when(tm == 0)
    def _():
        series_ref[0:tblocks, :] = jnp.zeros((tblocks, wide), F32)

    @pl.when(tm < n_tm - 1)
    def _():
        to_left.wait_recv()
        series_ref[2 * tblocks : 3 * tblocks, :] = halo_high[...].astype(F32)

    @pl.when(tm == n_tm - 1)
    def _():
        series_ref[2 * tblocks : 3 * tblocks, :] = jnp.zeros((tblocks, wide), F32)

    def make_frames(group, c):
        near = series_ref[pl.ds(pl.multiple_of(group * 8, 8), tblocks + 8), :]
        for r in range(8):
            rows = near[r : r + tblocks, :].astype(BF16)
            lanes = pl.ds(pl.multiple_of((group * 8 + r) * 128, 128), 128)
            for d in range(dets):
                frames_ref[d, :, lanes] = rows[:, d * 128 : (d + 1) * 128]
        return c

    lax.fori_loop(0, tap_rows // 8, make_frames, 0)
    end = series_ref[2 * tblocks : 3 * tblocks, :].astype(BF16)
    for d in range(dets):
        frames_ref[d, :, taps : taps + 128] = end[:, d * 128 : (d + 1) * 128]
    for d in range(dets):
        y_ref[:, d * 128 : (d + 1) * 128] = (
            dot(frames_ref[d], toep_ref[d], NT).astype(BF16).astype(F32)
        )

    def scan_bins(b, carry):
        rows = pl.ds(pl.multiple_of(b * per_block, per_block), per_block)
        mask = entry_mask(b)
        filtered = y_ref[pl.ds(b, 1), :]
        stack = [jnp.where(mask, filtered, 0.0)]
        for weight in (cos_ref, sin_ref):
            term = jnp.where(mask, filtered * weight[pl.ds(b, 1), :], 0.0)
            high = term.astype(BF16).astype(F32)
            stack += [high, term - high]
        stack.append(jnp.zeros((per_block, wide), F32))
        sums = dot(jnp.concatenate(stack, axis=0).astype(BF16), hot_ref[b], NT)
        g = per_block
        part_ref[0, rows, :] = sums[0:g]
        part_ref[1, rows, :] = sums[g : 2 * g] + sums[2 * g : 3 * g]
        part_ref[2, rows, :] = sums[3 * g : 4 * g] + sums[4 * g : 5 * g]
        return carry

    lax.fori_loop(0, tblocks, scan_bins, 0, unroll=4)

    outgoing = [quantize(part_ref[c]) for c in range(comps)]
    fill(ret_out, place_ref[...], outgoing, exponent_lanes([e for _, _, e in outgoing]))
    send_all(2, lambda d: ret_out.at[d], ret_in)
    ret_in[pl.ds(me, 1)] = ret_out[pl.ds(me, 1)]
    wait_all(2, lambda d: ret_out.at[d], ret_in)

    chosen = ask_in[...].reshape(slots, blocks)
    exps = ret_in[:, :, data : data + 128].reshape(slots, 128).astype(jnp.int32).astype(F32)
    totals = [jnp.zeros((1, 1), F32)] * 4
    for c in range(comps):
        high, low = split(ret_in[:, :, c * pixels : (c + 1) * pixels].reshape(slots, pixels))
        scale = jnp.exp2(exps[:, c : c + 1] - 15.0)
        image = dot(chosen, (high * (256.0 * scale)).astype(BF16), TN) + dot(
            chosen, (low * scale).astype(BF16), TN
        )
        image_ref[c] = image
        residual = r_ref[c]
        for i, product in enumerate(
            (residual * residual, p_ref[c] * image, residual * image, image * image)
        ):
            totals[i] = totals[i] + jnp.sum(product, keepdims=True)
    lane = iota((8, 128), 1)
    packed = jnp.zeros((8, 128), F32)
    for i in range(4):
        packed = jnp.where(lane == i, totals[i], packed)
    red_out[...] = packed
    red_in[pl.ds(me, 1)] = packed.reshape(1, 8, 128)
    send_all(3, lambda d: red_out, red_in)
    wait_all(3, lambda d: red_out, red_in)
    summed = jnp.sum(red_in[...], axis=0)[0:1, :]
    lane = iota((1, 128), 1)
    norm_old, curvature, cross, square = (
        jnp.sum(jnp.where(lane == i, summed, 0.0), axis=1, keepdims=True) for i in range(4)
    )
    step = norm_old / curvature
    norm_new = norm_old - 2.0 * step * cross + step * step * square
    ratio = norm_new / norm_old
    for c in range(comps):
        direction = p_ref[c]
        residual = r_ref[c] - step * image_ref[c]
        xo_ref[c] = x_ref[c] + step * direction
        ro_ref[c] = residual
        po_ref[c] = residual + ratio * direction

    wait_sent(0, lambda d: ask_out.at[d], ask_in)
    wait_sent(1, lambda d: ans_out.at[d], ans_in)
    wait_sent(2, lambda d: ret_out.at[d], ret_in)
    wait_sent(3, lambda d: red_out, red_in)

    @pl.when(tm < n_tm - 1)
    def _():
        to_right.wait_send()

    @pl.when(tm > 0)
    def _():
        to_left.wait_send()


def body(n_det, n_tm, x_map, r_map, p_map, pointing, pol_angle, noise_filter, block_list, block_home):
    n = n_det * n_tm
    comps, blocks, pixels = p_map.shape
    dets, samples = pointing.shape
    tblocks = block_list.shape[1]
    entries = tblocks * block_list.shape[2]
    taps = noise_filter.shape[1]
    cap = -(-(2 * entries // n) // 16) * 16
    slots = n * cap
    wide = dets * 128
    width = comps * pixels + 128
    assert samples == tblocks * 128 and taps == 2 * samples
    vmem = pltpu.VMEM
    out = jax.ShapeDtypeStruct(p_map.shape, F32)
    return pl.pallas_call(
        functools.partial(kernel, n_det, n_tm, cap),
        out_shape=(out, out, out),
        in_specs=[pl.BlockSpec(memory_space=vmem)] * 8,
        out_specs=[pl.BlockSpec(memory_space=vmem)] * 3,
        scratch_shapes=[
            vmem((n, cap, blocks), BF16),
            vmem((n, cap, blocks), BF16),
            vmem((n, cap, width), jnp.int16),
            vmem((n, cap, width), jnp.int16),
            vmem((n, cap, width), jnp.int16),
            vmem((n, cap, width), jnp.int16),
            vmem((8, 128), F32),
            vmem((n, 8, 128), F32),
            vmem((slots, entries), BF16),
            vmem((tblocks, pixels, wide), BF16),
            vmem((dets, 128, taps + 128), BF16),
            vmem((dets, tblocks, taps + 128), BF16),
            vmem((tblocks, wide), jnp.int32),
            vmem((tblocks, wide), F32),
            vmem((tblocks, wide), F32),
            vmem((tblocks, wide), F32),
            vmem((tblocks, wide), F32),
            vmem((3 * tblocks, wide), F32),
            vmem((tblocks, wide), BF16),
            vmem((tblocks, wide), BF16),
            vmem((tblocks, wide), BF16),
            vmem((comps, entries, pixels), F32),
            vmem((comps, entries, pixels), F32),
            vmem((comps, entries, pixels), F32),
            vmem((comps, blocks, pixels), F32),
            pltpu.SemaphoreType.DMA((4, n)),
            pltpu.SemaphoreType.DMA((4, n)),
            pltpu.SemaphoreType.DMA((2,)),
            pltpu.SemaphoreType.DMA((2,)),
        ],
        compiler_params=pltpu.CompilerParams(
            collective_id=0, has_side_effects=True, vmem_limit_bytes=60 * 1024 * 1024
        ),
    )(
        x_map, r_map, p_map, pointing, pol_angle, noise_filter,
        block_list.reshape(1, entries), block_home.reshape(-1, 128),
    )


def solution(mesh):
    maps = P(None, ("det", "tm"), None)
    return jax.shard_map(
        functools.partial(body, mesh.shape["det"], mesh.shape["tm"]),
        mesh=mesh,
        in_specs=(
            maps, maps, maps, P("det", "tm"), P("det", "tm"), P("det", None),
            P("det", "tm", None), P(),
        ),
        out_specs=(maps, maps, maps),
        check_vma=False,
    )
```

time: 706 us -> 90 us (0.13); the launches traced: 697 us -> 89.8 us
  local copies, waits for them, and re-layouts: 381 us -> 5.12 us
  other arithmetic: 107 us -> 0 us
  blocking collectives: 94.1 us -> 0 us
  waiting for transfers between devices: 92.4 us -> 0 us
  Pallas kernels: 0 us -> 84 us
  starting transfers between devices: 12.6 us -> 0 us
    gather x9 -> x0, local copies, waits for them, and re-layouts: 279 us -> none  [the longest x2 90.8 us: body(): local_map[0][address] + cosine * local_map[1][address]]
    scatter-add x1 -> x0, other arithmetic: 101 us -> none  [body(): jnp.zeros((3, per_device * pixels), jnp.float32).at[:, address.reshape(-1)]]
    all_to_all x2 -> x0, waiting for transfers between devices: 92.4 us -> none  [the longest x1 47.3 us: body(): lax.all_to_all(answer, ('det', 'tm'), split_axis=1, concat_axis=1, tiled=...]
    pallas_call x0 -> x1, Pallas kernels: none -> 84 us  [body(): pl.pallas_call(functools.partial(kernel, n_det, n_tm, cap), out_shape=(ou...]
    psum x2 -> x0, blocking collectives: 79.9 us -> none  [the longest x1 41.4 us: body(): norm_new = lax.psum(jnp.sum(r_next * r_next), ('det', 'tm'))]
    scatter x2 -> x0, local copies, waits for them, and re-layouts: 25.3 us -> none  [the longest x1 23.9 us: body(): outgoing = jnp.zeros((3, slot_count, pixels), jnp.float32).at[:, send_pla...]
    another operation x6 -> x0, local copies, waits for them, and re-layouts: 24.3 us -> none  [the longest x2 18.8 us: one_detector(): jnp.tile(extended, 128)[:128 * window_len].reshape(128, window_len)]
    unnamed x107 -> x8, local copies, waits for them, and re-layouts: 27.4 us -> 4.47 us
  transfers between devices with their start and end apart: 4 -> 0, of which waited for: 2 -> 0; matrix products, arithmetic and copies ran while one was open for 6% -> 0% of each run, Pallas kernels for 0% -> 0%
where the time goes in v1:
time: 90 us; the launch traced here: 89.8 us
  Pallas kernels  84 us (93%)
  local copies, waits for them, and re-layouts  5.12 us (6%)
    pallas_call x1, Pallas kernels, body(): pl.pallas_call(functools.partial(kernel, n_det, n_tm, cap), out_shape=(ou...  84 us
    unnamed x8, local copies, waits for them, and re-layouts  4.47 us

profile of v1, /device:TPU:0, one launch (start us, length us, event | category | flops | bytes accessed | tf_op | source)
XLA Modules:
  0.0 89.8 jit_solution(11579887504310575093)
XLA Ops:
  0.6 0.8 copy.12
  1.4 0.7 reshape.12.wanted_ref
  2.0 84.0 %shard_map.103 = (f32[3,128,256]{2,1,0:T(8,128)}, f32[3,128,256]{2,1,0:T(8,128)}, f32[3,128,256]{2,1,0:T(8,128)}) custom-call(f32[3,128,256]{2,1,0:T(8,128)} %x_ref.1, f32[3,128,256]{2,1,0:T(8,128)} %r_ref.1, f32[3,128,256]{2,1,0:T(8,128)} %p_ref.1, s32[4,4096]{1,0:T(4,128)} %point_ref.1, f32[4,4096]{1,0:T(4,128)} %angle_ref.1, bf16[4,8192]{1,0:T(4,128)(2,1)} %filter_ref.1, ...), custom_call_target="tpu_custom_call" | custom-call | tf_op jit(solution)/shard_map/pallas_call | solution.py:390
  86.0 0.0 copy-start.1
  86.1 1.8 %copy.16 = f32[3,128,256]{2,1,0:T(8,128)} copy(f32[3,128,256]{2,1,0:T(8,128)} %get-tuple-element.6) | data formatting | bytes 786432
  87.9 0.0 copy-done.1
  87.9 0.0 copy-start
  87.9 0.7 copy.17
  88.6 0.4 copy-done
  89.0 0.7 copy.18
Async XLA Ops:
  86.0 1.8 %copy-start.1 = (f32[3,128,256]{2,1,0:T(8,128)S(1)}, f32[3,128,256]{2,1,0:T(8,128)}, u32[]{:S(2)}) copy-start(f32[3,128,256]{2,1,0:T(8,128)} %get-tuple-element.7) | copy-start | bytes 1179652
  87.9 1.1 %copy-start = (f32[3,128,256]{2,1,0:T(8,128)S(1)}, f32[3,128,256]{2,1,0:T(8,128)}, u32[]{:S(2)}) copy-start(f32[3,128,256]{2,1,0:T(8,128)} %get-tuple-element.8) | copy-start | bytes 1179652

commit v2 on v1

--- a/solution.py
+++ b/solution.py
@@ -54,9 +54,10 @@
     x_ref, r_ref, p_ref, point_ref, angle_ref, filter_ref, wanted_ref, home_ref,
     xo_ref, ro_ref, po_ref,
     ask_out, ask_in, ans_out, ans_in, ret_out, ret_in, red_out, red_in,
+    ans_scale_out, ans_scale_in, ret_scale_out, ret_scale_in,
     place_ref, hot_ref, toep_ref, frames_ref, pt_ref, cos_ref, sin_ref, sig_ref, y_ref,
     series_ref, halo_out, halo_low, halo_high, lmh_ref, lml_ref, part_ref, image_ref,
-    send_sem, recv_sem, halo_send, halo_recv,
+    send_sem, recv_sem, red_send, red_recv, halo_send, halo_recv,
 ):
     n = n_det * n_tm
     det, tm = lax.axis_index("det"), lax.axis_index("tm")
@@ -69,8 +70,8 @@
     per_block = entries // tblocks
     taps = filter_ref.shape[1]
     tap_rows = taps // 128
+    half = n // 2
     wide = dets * 128
-    data = comps * pixels
 
     def device(index):
         return (index // n_tm, index % n_tm)
@@ -85,43 +86,35 @@
 
     lax.fori_loop(1, n, greet, 0)
 
-    def send_copy(stage, out, into, peer):
+    def send_all(*sends):
+        def start(peer):
+            for stage, source, into in sends:
+                pltpu.make_async_remote_copy(
+                    src_ref=source(peer), dst_ref=into.at[me], send_sem=send_sem.at[stage],
+                    recv_sem=recv_sem.at[stage], device_id=device(peer),
+                    device_id_type=pl.DeviceIdType.MESH,
+                ).start()
+
+        mine = (me // half) * half
+
+        def far(k, c):
+            start((mine + half) % n + (me + k) % half)
+            return c
+
+        def near(k, c):
+            start(mine + (me + k) % half)
+            return c
+
+        lax.fori_loop(0, half, far, 0)
+        lax.fori_loop(1, half, near, 0)
+
+    def everything(stage, buffer):
+        whole = buffer.at[pl.ds(0, n - 1)]
         return pltpu.make_async_remote_copy(
-            src_ref=out, dst_ref=into.at[me], send_sem=send_sem.at[stage, peer],
-            recv_sem=recv_sem.at[stage, me], device_id=device(peer),
+            src_ref=whole, dst_ref=whole, send_sem=send_sem.at[stage],
+            recv_sem=recv_sem.at[stage], device_id=device((me + 1) % n),
             device_id_type=pl.DeviceIdType.MESH,
         )
-
-    def recv_copy(stage, out, into, peer):
-        return pltpu.make_async_remote_copy(
-            src_ref=out, dst_ref=into.at[peer], send_sem=send_sem.at[stage, peer],
-            recv_sem=recv_sem.at[stage, peer], device_id=device(peer),
-            device_id_type=pl.DeviceIdType.MESH,
-        )
-
-    def send_all(stage, source, into):
-        def step(k, c):
-            peer = (me + k) % n
-            send_copy(stage, source(peer), into, peer).start()
-            return c
-
-        lax.fori_loop(1, n, step, 0)
-
-    def wait_all(stage, source, into):
-        def step(k, c):
-            peer = (me + n - k) % n
-            recv_copy(stage, source(peer), into, peer).wait_recv()
-            return c
-
-        lax.fori_loop(1, n, step, 0)
-
-    def wait_sent(stage, source, into):
-        def step(k, c):
-            peer = (me + k) % n
-            send_copy(stage, source(peer), into, peer).wait_send()
-            return c
-
-        lax.fori_loop(1, n, step, 0)
 
     wanted = wanted_ref[...]
     home = home_ref[...]
@@ -145,28 +138,48 @@
     slot_hot = onehot(iota((blocks, entries), 0) == slot)
     ask_out[...] = dot(place_ref[...], slot_hot, NT).astype(BF16).reshape(n, cap, blocks)
     pl.semaphore_wait(barrier, n - 1)
-    send_all(0, lambda d: ask_out.at[d], ask_in)
+    send_all((0, lambda d: ask_out.at[d], ask_in))
     ask_in[pl.ds(me, 1)] = ask_out[pl.ds(me, 1)]
 
     pieces = [quantize(p_ref[c]) for c in range(comps)]
     scales = exponent_lanes([e for _, _, e in pieces])
 
-    wait_all(0, lambda d: ask_out.at[d], ask_in)
+    everything(0, ask_in).wait_recv()
     asked = ask_in[...].reshape(slots, blocks)
 
     def place_words(selector, high, low):
         return (256.0 * dot(selector, high, NN) + dot(selector, low, NN)).astype(jnp.int32)
 
-    def fill(buffer, selector, quantized, scale_lanes):
+    shift = cap.bit_length() - 1
+    in_group = iota((slots, 128), 0) & (cap - 1)
+    spot = [iota((slots, 128), 1) == in_group + c * cap for c in range(comps)]
+    of_device = onehot((iota((n, slots), 1) >> shift) == iota((n, slots), 0))
+    device_of = onehot((iota((slots, n), 0) >> shift) == iota((slots, n), 1))
+
+    def slot_scales(buffer):
+        spread = dot(device_of, buffer[...].reshape(n, 128).astype(BF16), NN)
+        return [
+            jnp.exp2(jnp.sum(jnp.where(at, spread, 0.0), axis=1, keepdims=True) - 15.0)
+            for at in spot
+        ]
+
+    def fill(buffer, scale_buffer, selector, quantized, scale_lanes):
         for c, (high, low, _) in enumerate(quantized):
             words = place_words(selector, high, low).astype(jnp.int16)
             buffer[:, :, c * pixels : (c + 1) * pixels] = words.reshape(n, cap, pixels)
-        words = dot(selector, scale_lanes, NN).astype(jnp.int32).astype(jnp.int16)
-        buffer[:, :, data : data + 128] = words.reshape(n, cap, 128)
-
-    fill(ans_out, asked, pieces, scales)
-    send_all(1, lambda d: ans_out.at[d], ans_in)
+        picked = dot(selector, scale_lanes, NN)
+        row = jnp.zeros((slots, 128), F32)
+        for c in range(comps):
+            row = jnp.where(spot[c], picked[:, c : c + 1], row)
+        scale_buffer[...] = dot(of_device, row.astype(BF16), NN).reshape(n, 1, 128)
+
+    fill(ans_out, ans_scale_out, asked, pieces, scales)
+    send_all(
+        (3, lambda d: ans_scale_out.at[d], ans_scale_in),
+        (1, lambda d: ans_out.at[d], ans_in),
+    )
     ans_in[pl.ds(me, 1)] = ans_out[pl.ds(me, 1)]
+    ans_scale_in[pl.ds(me, 1)] = ans_scale_out[pl.ds(me, 1)]
 
     for b in range(tblocks):
         for d in range(dets):
@@ -204,16 +217,16 @@
     for d in range(dets):
         toep_ref[d, :, taps : taps + 128] = jnp.where(upper, 0.0, last[d]).astype(BF16)
 
-    wait_all(1, lambda d: ans_out.at[d], ans_in)
-
-    words = ans_in[:, :, data : data + 128].reshape(slots, 128)
+    everything(1, ans_in).wait_recv()
+    everything(3, ans_scale_in).wait_recv()
+
     place = place_ref[...]
-    exps = dot(place, words.astype(jnp.int32).astype(F32).astype(BF16), TN)
+    scales_in = slot_scales(ans_scale_in)
     for c in range(comps):
         high, low = split(ans_in[:, :, c * pixels : (c + 1) * pixels].reshape(slots, pixels))
-        scale = jnp.exp2(exps[:, c : c + 1] - 15.0)
-        lmh_ref[c] = dot(place, high.astype(BF16), TN) * (256.0 * scale)
-        lml_ref[c] = dot(place, low.astype(BF16), TN) * scale
+        scale = scales_in[c]
+        lmh_ref[c] = dot(place, (high * (256.0 * scale)).astype(BF16), TN)
+        lml_ref[c] = dot(place, (low * scale).astype(BF16), TN)
 
     def entry_mask(b):
         return iota((per_block, wide), 0) == (pt_ref[pl.ds(b, 1), :] // pixels)
@@ -316,17 +329,22 @@
     lax.fori_loop(0, tblocks, scan_bins, 0, unroll=4)
 
     outgoing = [quantize(part_ref[c]) for c in range(comps)]
-    fill(ret_out, place_ref[...], outgoing, exponent_lanes([e for _, _, e in outgoing]))
-    send_all(2, lambda d: ret_out.at[d], ret_in)
+    fill(ret_out, ret_scale_out, place_ref[...], outgoing, exponent_lanes([e for _, _, e in outgoing]))
+    send_all(
+        (4, lambda d: ret_scale_out.at[d], ret_scale_in),
+        (2, lambda d: ret_out.at[d], ret_in),
+    )
     ret_in[pl.ds(me, 1)] = ret_out[pl.ds(me, 1)]
-    wait_all(2, lambda d: ret_out.at[d], ret_in)
+    ret_scale_in[pl.ds(me, 1)] = ret_scale_out[pl.ds(me, 1)]
+    everything(2, ret_in).wait_recv()
+    everything(4, ret_scale_in).wait_recv()
 
     chosen = ask_in[...].reshape(slots, blocks)
-    exps = ret_in[:, :, data : data + 128].reshape(slots, 128).astype(jnp.int32).astype(F32)
+    scales_in = slot_scales(ret_scale_in)
     totals = [jnp.zeros((1, 1), F32)] * 4
     for c in range(comps):
         high, low = split(ret_in[:, :, c * pixels : (c + 1) * pixels].reshape(slots, pixels))
-        scale = jnp.exp2(exps[:, c : c + 1] - 15.0)
+        scale = scales_in[c]
         image = dot(chosen, (high * (256.0 * scale)).astype(BF16), TN) + dot(
             chosen, (low * scale).astype(BF16), TN
         )
@@ -340,11 +358,28 @@
     packed = jnp.zeros((8, 128), F32)
     for i in range(4):
         packed = jnp.where(lane == i, totals[i], packed)
-    red_out[...] = packed
-    red_in[pl.ds(me, 1)] = packed.reshape(1, 8, 128)
-    send_all(3, lambda d: red_out, red_in)
-    wait_all(3, lambda d: red_out, red_in)
-    summed = jnp.sum(red_in[...], axis=0)[0:1, :]
+    red_out[0] = packed
+
+    def share(level, own, count, target):
+        def copy(slot, peer):
+            return pltpu.make_async_remote_copy(
+                src_ref=red_out.at[level], dst_ref=red_in.at[level, slot],
+                send_sem=red_send.at[level, peer], recv_sem=red_recv.at[level, slot],
+                device_id=target(peer), device_id_type=pl.DeviceIdType.MESH,
+            )
+
+        for k in range(1, count):
+            copy(own, (own + k) % count).start()
+        red_in[level, pl.ds(own, 1)] = red_out[level].reshape(1, 8, 128)
+        for k in range(1, count):
+            peer = (own + count - k) % count
+            copy(peer, peer).wait_recv()
+        return jnp.sum(red_in[level, 0:count], axis=0), copy
+
+    row_sum, row_copy = share(0, tm, n_tm, lambda peer: (det, peer))
+    red_out[1] = row_sum
+    full_sum, column_copy = share(1, det, n_det, lambda peer: (peer, tm))
+    summed = full_sum[0:1, :]
     lane = iota((1, 128), 1)
     norm_old, curvature, cross, square = (
         jnp.sum(jnp.where(lane == i, summed, 0.0), axis=1, keepdims=True) for i in range(4)
@@ -359,10 +394,14 @@
         ro_ref[c] = residual
         po_ref[c] = residual + ratio * direction
 
-    wait_sent(0, lambda d: ask_out.at[d], ask_in)
-    wait_sent(1, lambda d: ans_out.at[d], ans_in)
-    wait_sent(2, lambda d: ret_out.at[d], ret_in)
-    wait_sent(3, lambda d: red_out, red_in)
+    everything(0, ask_out).wait_send()
+    everything(1, ans_out).wait_send()
+    everything(3, ans_scale_out).wait_send()
+    everything(2, ret_out).wait_send()
+    everything(4, ret_scale_out).wait_send()
+    for copy, own, count in ((row_copy, tm, n_tm), (column_copy, det, n_det)):
+        for k in range(1, count):
+            copy(own, (own + k) % count).wait_send()
 
     @pl.when(tm < n_tm - 1)
     def _():
@@ -383,7 +422,8 @@
     cap = -(-(2 * entries // n) // 16) * 16
     slots = n * cap
     wide = dets * 128
-    width = comps * pixels + 128
+    width = comps * pixels
+    assert cap & (cap - 1) == 0 and 3 * cap <= 128
     assert samples == tblocks * 128 and taps == 2 * samples
     vmem = pltpu.VMEM
     out = jax.ShapeDtypeStruct(p_map.shape, F32)
@@ -399,8 +439,12 @@
             vmem((n, cap, width), jnp.int16),
             vmem((n, cap, width), jnp.int16),
             vmem((n, cap, width), jnp.int16),
-            vmem((8, 128), F32),
-            vmem((n, 8, 128), F32),
+            vmem((2, 8, 128), F32),
+            vmem((2, max(n_det, n_tm), 8, 128), F32),
+            vmem((n, 1, 128), F32),
+            vmem((n, 1, 128), F32),
+            vmem((n, 1, 128), F32),
+            vmem((n, 1, 128), F32),
             vmem((slots, entries), BF16),
             vmem((tblocks, pixels, wide), BF16),
             vmem((dets, 128, taps + 128), BF16),
@@ -418,8 +462,10 @@
             vmem((comps, entries, pixels), F32),
             vmem((comps, entries, pixels), F32),
             vmem((comps, blocks, pixels), F32),
-            pltpu.SemaphoreType.DMA((4, n)),
-            pltpu.SemaphoreType.DMA((4, n)),
+            pltpu.SemaphoreType.DMA((5,)),
+            pltpu.SemaphoreType.DMA((5,)),
+            pltpu.SemaphoreType.DMA((2, max(n_det, n_tm))),
+            pltpu.SemaphoreType.DMA((2, max(n_det, n_tm))),
             pltpu.SemaphoreType.DMA((2,)),
             pltpu.SemaphoreType.DMA((2,)),
         ],

time: 90 us -> 80.4 us (0.89)
  Pallas kernels: 84 us -> 74.4 us
    pallas_call x1, Pallas kernels: 84 us -> 74.4 us  [body(): pl.pallas_call(functools.partial(kernel, n_det, n_tm, cap), out_shape=(ou...]
where the time goes in v2:
time: 80.4 us; the launch traced here: 80.1 us
  Pallas kernels  74.4 us (93%)
  local copies, waits for them, and re-layouts  5.12 us (6%)
    pallas_call x1, Pallas kernels, body(): pl.pallas_call(functools.partial(kernel, n_det, n_tm, cap), out_shape=(ou...  74.4 us
    unnamed x8, local copies, waits for them, and re-layouts  4.47 us

profile of v2, /device:TPU:0, one launch (start us, length us, event | category | flops | bytes accessed | tf_op | source)
XLA Modules:
  0.0 80.1 jit_solution(7619521667774774300)
XLA Ops:
  0.6 0.8 copy.12
  1.4 0.7 reshape.12.wanted_ref
  2.0 74.4 %shard_map.103 = (f32[3,128,256]{2,1,0:T(8,128)}, f32[3,128,256]{2,1,0:T(8,128)}, f32[3,128,256]{2,1,0:T(8,128)}) custom-call(f32[3,128,256]{2,1,0:T(8,128)} %x_ref.1, f32[3,128,256]{2,1,0:T(8,128)} %r_ref.1, f32[3,128,256]{2,1,0:T(8,128)} %p_ref.1, s32[4,4096]{1,0:T(4,128)} %point_ref.1, f32[4,4096]{1,0:T(4,128)} %angle_ref.1, bf16[4,8192]{1,0:T(4,128)(2,1)} %filter_ref.1, ...), custom_call_target="tpu_custom_call" | custom-call | tf_op jit(solution)/shard_map/pallas_call | solution.py:430
  76.4 0.0 copy-start.1
  76.4 1.8 %copy.16 = f32[3,128,256]{2,1,0:T(8,128)} copy(f32[3,128,256]{2,1,0:T(8,128)} %get-tuple-element.6) | data formatting | bytes 786432
  78.3 0.0 copy-done.1
  78.3 0.0 copy-start
  78.3 0.7 copy.17
  79.0 0.4 copy-done
  79.4 0.7 copy.18
Async XLA Ops:
  76.4 1.8 %copy-start.1 = (f32[3,128,256]{2,1,0:T(8,128)S(1)}, f32[3,128,256]{2,1,0:T(8,128)}, u32[]{:S(2)}) copy-start(f32[3,128,256]{2,1,0:T(8,128)} %get-tuple-element.7) | copy-start | bytes 1179652
  78.3 1.1 %copy-start = (f32[3,128,256]{2,1,0:T(8,128)S(1)}, f32[3,128,256]{2,1,0:T(8,128)}, u32[]{:S(2)}) copy-start(f32[3,128,256]{2,1,0:T(8,128)} %get-tuple-element.8) | copy-start | bytes 1179652

commit v3 on v2

--- a/solution.py
+++ b/solution.py
@@ -55,7 +55,7 @@
     xo_ref, ro_ref, po_ref,
     ask_out, ask_in, ans_out, ans_in, ret_out, ret_in, red_out, red_in,
     ans_scale_out, ans_scale_in, ret_scale_out, ret_scale_in,
-    place_ref, hot_ref, toep_ref, frames_ref, pt_ref, cos_ref, sin_ref, sig_ref, y_ref,
+    asked_ref, place_ref, hot_ref, toep_ref, frames_ref, pt_ref, cos_ref, sin_ref, sig_ref, y_ref,
     series_ref, halo_out, halo_low, halo_high, lmh_ref, lml_ref, part_ref, image_ref,
     send_sem, recv_sem, red_send, red_recv, halo_send, halo_recv,
 ):
@@ -136,25 +136,29 @@
     ).astype(jnp.int32)
     place_ref[...] = onehot(iota((slots, entries), 0) == owner * cap + rank)
     slot_hot = onehot(iota((blocks, entries), 0) == slot)
-    ask_out[...] = dot(place_ref[...], slot_hot, NT).astype(BF16).reshape(n, cap, blocks)
-    pl.semaphore_wait(barrier, n - 1)
-    send_all((0, lambda d: ask_out.at[d], ask_in))
-    ask_in[pl.ds(me, 1)] = ask_out[pl.ds(me, 1)]
-
-    pieces = [quantize(p_ref[c]) for c in range(comps)]
-    scales = exponent_lanes([e for _, _, e in pieces])
-
-    everything(0, ask_in).wait_recv()
-    asked = ask_in[...].reshape(slots, blocks)
-
-    def place_words(selector, high, low):
-        return (256.0 * dot(selector, high, NN) + dot(selector, low, NN)).astype(jnp.int32)
-
     shift = cap.bit_length() - 1
     in_group = iota((slots, 128), 0) & (cap - 1)
     spot = [iota((slots, 128), 1) == in_group + c * cap for c in range(comps)]
     of_device = onehot((iota((n, slots), 1) >> shift) == iota((n, slots), 0))
     device_of = onehot((iota((slots, n), 0) >> shift) == iota((slots, n), 1))
+    named = dot(place_ref[...], slot_hot, NT) * (iota((slots, blocks), 1) + 1).astype(F32)
+    named = jnp.where(spot[0], jnp.sum(named, axis=1, keepdims=True), 0.0).astype(BF16)
+    ask_out[...] = dot(of_device, named, NN).reshape(n, 1, 128)
+    pl.semaphore_wait(barrier, n - 1)
+    send_all((0, lambda d: ask_out.at[d], ask_in))
+    ask_in[pl.ds(me, 1)] = ask_out[pl.ds(me, 1)]
+
+    pieces = [quantize(p_ref[c]) for c in range(comps)]
+    scales = exponent_lanes([e for _, _, e in pieces])
+
+    everything(0, ask_in).wait_recv()
+    spread = dot(device_of, ask_in[...].reshape(n, 128).astype(BF16), NN)
+    name = jnp.sum(jnp.where(spot[0], spread, 0.0), axis=1, keepdims=True).astype(jnp.int32)
+    asked = onehot(iota((slots, blocks), 1) + 1 == name)
+    asked_ref[...] = asked
+
+    def place_words(selector, high, low):
+        return (256.0 * dot(selector, high, NN) + dot(selector, low, NN)).astype(jnp.int32)
 
     def slot_scales(buffer):
         spread = dot(device_of, buffer[...].reshape(n, 128).astype(BF16), NN)
@@ -163,23 +167,25 @@
             for at in spot
         ]
 
-    def fill(buffer, scale_buffer, selector, quantized, scale_lanes):
-        for c, (high, low, _) in enumerate(quantized):
-            words = place_words(selector, high, low).astype(jnp.int16)
-            buffer[:, :, c * pixels : (c + 1) * pixels] = words.reshape(n, cap, pixels)
+    def fill_and_send(out, into, scale_out, scale_in, stage, selector, quantized, scale_lanes):
         picked = dot(selector, scale_lanes, NN)
         row = jnp.zeros((slots, 128), F32)
         for c in range(comps):
             row = jnp.where(spot[c], picked[:, c : c + 1], row)
-        scale_buffer[...] = dot(of_device, row.astype(BF16), NN).reshape(n, 1, 128)
-
-    fill(ans_out, ans_scale_out, asked, pieces, scales)
-    send_all(
-        (3, lambda d: ans_scale_out.at[d], ans_scale_in),
-        (1, lambda d: ans_out.at[d], ans_in),
+        scale_out[...] = dot(of_device, row.astype(BF16), NN).reshape(n, 1, 128)
+        scale_in[pl.ds(me, 1)] = scale_out[pl.ds(me, 1)]
+        sends = [(stage, lambda d: scale_out.at[d], scale_in)]
+        for c, (high, low, _) in enumerate(quantized):
+            words = place_words(selector, high, low).astype(jnp.int16)
+            out[c] = words.reshape(n, cap, pixels)
+            sends.append((stage + 1 + c, lambda d, c=c: out.at[c, d], into.at[c]))
+            send_all(*sends)
+            sends = []
+            into[c, pl.ds(me, 1)] = out[c, pl.ds(me, 1)]
+
+    fill_and_send(
+        ans_out, ans_in, ans_scale_out, ans_scale_in, 1, asked, pieces, scales,
     )
-    ans_in[pl.ds(me, 1)] = ans_out[pl.ds(me, 1)]
-    ans_scale_in[pl.ds(me, 1)] = ans_scale_out[pl.ds(me, 1)]
 
     for b in range(tblocks):
         for d in range(dets):
@@ -217,13 +223,13 @@
     for d in range(dets):
         toep_ref[d, :, taps : taps + 128] = jnp.where(upper, 0.0, last[d]).astype(BF16)
 
-    everything(1, ans_in).wait_recv()
-    everything(3, ans_scale_in).wait_recv()
+    everything(1, ans_scale_in).wait_recv()
 
     place = place_ref[...]
     scales_in = slot_scales(ans_scale_in)
     for c in range(comps):
-        high, low = split(ans_in[:, :, c * pixels : (c + 1) * pixels].reshape(slots, pixels))
+        everything(1 + 1 + c, ans_in.at[c]).wait_recv()
+        high, low = split(ans_in[c].reshape(slots, pixels))
         scale = scales_in[c]
         lmh_ref[c] = dot(place, (high * (256.0 * scale)).astype(BF16), TN)
         lml_ref[c] = dot(place, (low * scale).astype(BF16), TN)
@@ -329,21 +335,18 @@
     lax.fori_loop(0, tblocks, scan_bins, 0, unroll=4)
 
     outgoing = [quantize(part_ref[c]) for c in range(comps)]
-    fill(ret_out, ret_scale_out, place_ref[...], outgoing, exponent_lanes([e for _, _, e in outgoing]))
-    send_all(
-        (4, lambda d: ret_scale_out.at[d], ret_scale_in),
-        (2, lambda d: ret_out.at[d], ret_in),
+    fill_and_send(
+        ret_out, ret_in, ret_scale_out, ret_scale_in, 5, place_ref[...], outgoing,
+        exponent_lanes([e for _, _, e in outgoing]),
     )
-    ret_in[pl.ds(me, 1)] = ret_out[pl.ds(me, 1)]
-    ret_scale_in[pl.ds(me, 1)] = ret_scale_out[pl.ds(me, 1)]
-    everything(2, ret_in).wait_recv()
-    everything(4, ret_scale_in).wait_recv()
-
-    chosen = ask_in[...].reshape(slots, blocks)
+    everything(5, ret_scale_in).wait_recv()
+
+    chosen = asked_ref[...]
     scales_in = slot_scales(ret_scale_in)
     totals = [jnp.zeros((1, 1), F32)] * 4
     for c in range(comps):
-        high, low = split(ret_in[:, :, c * pixels : (c + 1) * pixels].reshape(slots, pixels))
+        everything(5 + 1 + c, ret_in.at[c]).wait_recv()
+        high, low = split(ret_in[c].reshape(slots, pixels))
         scale = scales_in[c]
         image = dot(chosen, (high * (256.0 * scale)).astype(BF16), TN) + dot(
             chosen, (low * scale).astype(BF16), TN
@@ -395,10 +398,12 @@
         po_ref[c] = residual + ratio * direction
 
     everything(0, ask_out).wait_send()
-    everything(1, ans_out).wait_send()
-    everything(3, ans_scale_out).wait_send()
-    everything(2, ret_out).wait_send()
-    everything(4, ret_scale_out).wait_send()
+    for c in range(comps):
+        everything(1 + 1 + c, ans_out.at[c]).wait_send()
+    everything(1, ans_scale_out).wait_send()
+    for c in range(comps):
+        everything(5 + 1 + c, ret_out.at[c]).wait_send()
+    everything(5, ret_scale_out).wait_send()
     for copy, own, count in ((row_copy, tm, n_tm), (column_copy, det, n_det)):
         for k in range(1, count):
             copy(own, (own + k) % count).wait_send()
@@ -422,8 +427,7 @@
     cap = -(-(2 * entries // n) // 16) * 16
     slots = n * cap
     wide = dets * 128
-    width = comps * pixels
-    assert cap & (cap - 1) == 0 and 3 * cap <= 128
+    assert cap & (cap - 1) == 0 and 3 * cap <= 128 and blocks < 256
     assert samples == tblocks * 128 and taps == 2 * samples
     vmem = pltpu.VMEM
     out = jax.ShapeDtypeStruct(p_map.shape, F32)
@@ -433,18 +437,19 @@
         in_specs=[pl.BlockSpec(memory_space=vmem)] * 8,
         out_specs=[pl.BlockSpec(memory_space=vmem)] * 3,
         scratch_shapes=[
-            vmem((n, cap, blocks), BF16),
-            vmem((n, cap, blocks), BF16),
-            vmem((n, cap, width), jnp.int16),
-            vmem((n, cap, width), jnp.int16),
-            vmem((n, cap, width), jnp.int16),
-            vmem((n, cap, width), jnp.int16),
+            vmem((n, 1, 128), F32),
+            vmem((n, 1, 128), F32),
+            vmem((comps, n, cap, pixels), jnp.int16),
+            vmem((comps, n, cap, pixels), jnp.int16),
+            vmem((comps, n, cap, pixels), jnp.int16),
+            vmem((comps, n, cap, pixels), jnp.int16),
             vmem((2, 8, 128), F32),
             vmem((2, max(n_det, n_tm), 8, 128), F32),
             vmem((n, 1, 128), F32),
             vmem((n, 1, 128), F32),
             vmem((n, 1, 128), F32),
             vmem((n, 1, 128), F32),
+            vmem((slots, blocks), BF16),
             vmem((slots, entries), BF16),
             vmem((tblocks, pixels, wide), BF16),
             vmem((dets, 128, taps + 128), BF16),
@@ -462,8 +467,8 @@
             vmem((comps, entries, pixels), F32),
             vmem((comps, entries, pixels), F32),
             vmem((comps, blocks, pixels), F32),
-            pltpu.SemaphoreType.DMA((5,)),
-            pltpu.SemaphoreType.DMA((5,)),
+            pltpu.SemaphoreType.DMA((9,)),
+            pltpu.SemaphoreType.DMA((9,)),
             pltpu.SemaphoreType.DMA((2, max(n_det, n_tm))),
             pltpu.SemaphoreType.DMA((2, max(n_det, n_tm))),
             pltpu.SemaphoreType.DMA((2,)),

time: 80.4 us -> 78.9 us (0.981)
  Pallas kernels: 74.4 us -> 72.9 us
    pallas_call x1, Pallas kernels: 74.4 us -> 72.9 us  [body(): pl.pallas_call(functools.partial(kernel, n_det, n_tm, cap), out_shape=(ou...]
where the time goes in v3:
time: 78.9 us; the launch traced here: 78.6 us
  Pallas kernels  72.9 us (92%)
  local copies, waits for them, and re-layouts  5.12 us (6%)
    pallas_call x1, Pallas kernels, body(): pl.pallas_call(functools.partial(kernel, n_det, n_tm, cap), out_shape=(ou...  72.9 us
    unnamed x8, local copies, waits for them, and re-layouts  4.47 us

profile of v3, /device:TPU:0, one launch (start us, length us, event | category | flops | bytes accessed | tf_op | source)
XLA Modules:
  0.0 78.6 jit_solution(8329561083787723560)
XLA Ops:
  0.6 0.8 copy.12
  1.4 0.7 reshape.12.wanted_ref
  2.0 72.9 %shard_map.103 = (f32[3,128,256]{2,1,0:T(8,128)}, f32[3,128,256]{2,1,0:T(8,128)}, f32[3,128,256]{2,1,0:T(8,128)}) custom-call(f32[3,128,256]{2,1,0:T(8,128)} %x_ref.1, f32[3,128,256]{2,1,0:T(8,128)} %r_ref.1, f32[3,128,256]{2,1,0:T(8,128)} %p_ref.1, s32[4,4096]{1,0:T(4,128)} %point_ref.1, f32[4,4096]{1,0:T(4,128)} %angle_ref.1, bf16[4,8192]{1,0:T(4,128)(2,1)} %filter_ref.1, ...), custom_call_target="tpu_custom_call" | custom-call | tf_op jit(solution)/shard_map/pallas_call | solution.py:434
  74.9 0.0 copy-start.1
  74.9 1.8 %copy.16 = f32[3,128,256]{2,1,0:T(8,128)} copy(f32[3,128,256]{2,1,0:T(8,128)} %get-tuple-element.6) | data formatting | bytes 786432
  76.8 0.0 copy-done.1
  76.8 0.0 copy-start
  76.8 0.7 copy.17
  77.5 0.4 copy-done
  77.9 0.7 copy.18
Async XLA Ops:
  74.9 1.8 %copy-start.1 = (f32[3,128,256]{2,1,0:T(8,128)S(1)}, f32[3,128,256]{2,1,0:T(8,128)}, u32[]{:S(2)}) copy-start(f32[3,128,256]{2,1,0:T(8,128)} %get-tuple-element.7) | copy-start | bytes 1179652
  76.8 1.1 %copy-start = (f32[3,128,256]{2,1,0:T(8,128)S(1)}, f32[3,128,256]{2,1,0:T(8,128)}, u32[]{:S(2)}) copy-start(f32[3,128,256]{2,1,0:T(8,128)} %get-tuple-element.8) | copy-start | bytes 1179652
